TPU v7x, 32 devices: a whole 2x2x4 slice. The times are simulated.
32 devices in a mesh: mp: 8 (over z, y), dp: 4 (over x, core).
Axes of the slice: x: 2, y: 2, z: 4, core: 2. Of those that a mesh axis runs over, the one named last changes fastest.
Arguments:
- momentum: float32 [8192, 28672], P('mp', 'dp'), may hold values from -120 to 120, as said below
- gradient: bfloat16 [8192, 28672], P('mp', 'dp'), may hold values from -4 to 4
- factor_q: bfloat16 [28672, 128], P(('dp', 'mp')), may hold values from -0.03125 to 0.03125
Outputs:
- momentum_out: float32 [8192, 28672], P('mp', 'dp')
- factor_out: bfloat16 [28672, 128], P(('dp', 'mp'))
- update: bfloat16 [8192, 28672], P('mp', 'dp')
Inputs may be any that keep to these rules, and one draw needn't show every extreme that they name: `momentum`: entries are finite reals.
All inputs are finite; a program needn't handle non-finite values.
Results may differ from a plain program's by a relative error of at most 0.00135.
Values may be sent and summed in bfloat16 or wider, within the bound.
A program may use at most 192 MiB of HBM per device.

v0:
```python
import math

import jax
import jax.numpy as jnp
from jax import lax
from jax.sharding import PartitionSpec as P

D = 8192
FF = 28672
RANK = 128


highest = lax.Precision.HIGHEST
feedback_rate = 0.05


def make_orthonormal(power_left, gram_matrix):
    factor_low = jnp.linalg.cholesky(gram_matrix)
    return jax.scipy.linalg.solve_triangular(factor_low, power_left.T, lower=True).T


def local(momentum, gradient, factor_q):
    blended = momentum + gradient.astype(jnp.float32)
    cols_local = blended.shape[1]
    share_rows = cols_local // lax.axis_size("mp")
    columns = blended
    power_part = jnp.dot(
        columns,
        lax.all_gather(factor_q, "mp", axis=0, tiled=True).astype(jnp.float32),
        precision=highest,
    )
    power_left = lax.psum(power_part, "dp")
    gram_matrix = lax.psum(jnp.dot(power_left.T, power_left, precision=highest), "mp")
    orthonormal = make_orthonormal(power_left, gram_matrix)
    columns = blended
    right_share = lax.psum_scatter(
        jnp.dot(columns.T, orthonormal, precision=highest), "mp", scatter_dimension=0, tiled=True
    )
    column_sums = lax.psum(jnp.sum(right_share * right_share, axis=0), ("mp", "dp"))
    power_right = lax.all_gather(right_share, "mp", axis=0, tiled=True)
    q_new = power_right * lax.rsqrt(column_sums + 1e-06)
    q_share = lax.dynamic_slice_in_dim(q_new, lax.axis_index("mp") * share_rows, share_rows, 0)
    momentum_out = blended - feedback_rate * jnp.dot(orthonormal, power_right.T, precision=highest)
    scale_factor = math.sqrt(D * FF / RANK)
    update = (scale_factor * jnp.dot(orthonormal, q_new.T, precision=highest)).astype(jnp.bfloat16)
    return (momentum_out, q_share.astype(jnp.bfloat16), update)


def solution(mesh):
    return jax.shard_map(
        local,
        mesh=mesh,
        in_specs=(P("mp", "dp"), P("mp", "dp"), P(("dp", "mp"), None)),
        out_specs=(P("mp", "dp"), P(("dp", "mp"), None), P("mp", "dp")),
        check_vma=False,
    )
```

profile of v0, /device:TPU:0, one launch (start us, length us, event | category | flops | bytes accessed | tf_op | source)
XLA Modules:
  0.0 484.5 jit_solution(17248685713365621945)
XLA Ops:
  7.2 0.0 all-gather.3.cloned.1.call-start
  7.2 0.7 all-gather.3.cloned.1.call-update
  7.9 0.0 all-reduce.3.cloned.1.call-start
  7.9 51.2 %all-gather.3.cloned.1.call-done = bf16[7168,128]{1,0:T(8,128)(2,1)} async-done(((bf16[896,128]{1,0:T(8,128)(2,1)}), bf16[7168,128]{1,0:T(8,128)(2,1)}) %all-gather.3.cloned.1.call-update) | async-done | bytes 1835024 | tf_op jit(solution)/shard_map/all_gather | solution.py:29
  59.2 21.4 %fusion.1 = f32[1024,128]{1,0:T(8,128)} fusion(bf16[7168,128]{1,0:T(8,128)(2,1)} %all-gather.3.cloned.1.call-done, f32[1024,7168]{1,0:T(8,128)} %param.3, bf16[1024,7168]{1,0:T(8,128)(2,1)} %param.4), kind=kOutput, calls=%fused_computation.4 | convolution fusion | flops 11288969216 | bytes 46399488 | tf_op jit(solution)/shard_map/dot_general | solution.py:27
  80.6 0.0 all-reduce.3.cloned.1.call-update
  80.6 0.0 all-reduce.5.cloned.1.call-start
  80.6 32.3 %all-reduce.3.cloned.1.call-done = f32[1024,128]{1,0:T(8,128)} async-done(((f32[1024,128]{1,0:T(8,128)}), f32[1024,128]{1,0:T(8,128)}) %all-reduce.3.cloned.1.call-update) | async-done | bytes 524304 | tf_op jit(solution)/shard_map/psum | solution.py:32
  113.0 2.8 fusion.6
  115.8 0.0 all-reduce.5.cloned.1.call-update
  115.8 0.6 reduce-scatter.2.cloned.1.call-start
  116.4 69.1 %all-reduce.5.cloned.1.call-done = f32[128,128]{0,1:T(8,128)} async-done(((f32[128,128]{0,1:T(8,128)}), f32[128,128]{0,1:T(8,128)}) %all-reduce.5.cloned.1.call-update) | async-done | bytes 65552 | tf_op jit(solution)/shard_map/psum | solution.py:33
  185.5 0.9 copy.7
  186.4 0.9 fusion.5
  187.3 11.7 %cholesky.16 = f32[128,128]{1,0:T(8,128)S(1)} custom-call(f32[128,128]{1,0:T(8,128)S(1)} %fusion.5), custom_call_target="Cholesky" | custom-call | tf_op jit(solution)/shard_map/jit(cholesky)/cholesky | solution.py:18
  199.0 0.6 compare_reduce_fusion
  199.7 0.7 fusion.2
  200.3 9.8 %custom-call.7 = f32[1,128,128]{1,2,0:T(8,128)S(1)} custom-call(f32[1,128,128]{2,1,0:T(8,128)S(1)} %fusion.2), custom_call_target="InvertDiagBlocksLowerTriangular" | custom-call | tf_op jit(solution)/shard_map/jit(_solve_triangular)/triangular_solve | solution.py:19
  210.1 1.7 fusion.3
  211.8 51.6 %fusion = f32[7168,128]{1,0:T(8,128)} fusion(f32[128,1024]{1,0:T(8,128)S(1)} %fusion.3, f32[1024,7168]{1,0:T(8,128)} %param.3, bf16[1024,7168]{1,0:T(8,128)(2,1)} %param.4), kind=kOutput, calls=%fused_computation.3 | convolution fusion | flops 11288969216 | bytes 48234496 | tf_op jit(solution)/shard_map/dot_general | solution.py:37
  263.4 0.0 reduce-scatter.2.cloned.1.call-update
  263.5 0.3 all-gather.5.cloned.1.call-start
  263.7 80.7 %reduce-scatter.2.cloned.1.call-done = f32[896,128]{1,0:T(8,128)} async-done(((f32[7168,128]{1,0:T(8,128)}), f32[896,128]{1,0:T(8,128)}) %reduce-scatter.2.cloned.1.call-update) | async-done | bytes 458768 | tf_op jit(solution)/shard_map/reduce_scatter | solution.py:36
  344.4 0.0 all-gather.5.cloned.1.call-update
  344.4 1.2 multiply_reduce_fusion
  345.6 41.2 %psum.23 = f32[128]{0:T(128)S(1)} all-reduce(f32[128]{0:T(128)S(1)} %multiply_reduce_fusion), channel_id=1, replica_groups=mesh['mp'=8,'dp'=4] {'mp','dp'}, use_global_device_ids=true, to_apply=%region_6.7 | all-reduce | flops 128 | bytes 1024 | tf_op jit(solution)/shard_map/psum | solution.py:39
  386.8 27.6 %all-gather.5.cloned.1.call-done = f32[7168,128]{1,0:T(8,128)} async-done(((f32[896,128]{1,0:T(8,128)}), f32[7168,128]{1,0:T(8,128)}) %all-gather.5.cloned.1.call-update) | async-done | bytes 3670032 | tf_op jit(solution)/shard_map/all_gather | solution.py:40
  414.5 0.0 copy-start
  414.5 2.4 broadcast_multiply_fusion
  416.9 25.9 %multiply_convert_fusion = bf16[1024,7168]{1,0:T(8,128)(2,1)} fusion(f32[128,1024]{1,0:T(8,128)S(1)} %fusion.3, f32[7168,128]{1,0:T(8,128)S(1)} %broadcast_multiply_fusion), kind=kOutput, calls=%fused_computation | convolution fusion | flops 11288969216 | bytes 18874368 | tf_op jit(solution)/shard_map/dot_general | solution.py:45
  442.8 0.7 dynamic-slice_convert_fusion
  443.5 0.0 copy-done
  443.5 34.2 %multiply_subtract_fusion = f32[1024,7168]{1,0:T(8,128)} fusion(f32[128,1024]{1,0:T(8,128)S(1)} %fusion.3, f32[7168,128]{1,0:T(8,128)S(1)} %copy-done, f32[1024,7168]{1,0:T(8,128)} %param.3, bf16[1024,7168]{1,0:T(8,128)(2,1)} %param.4), kind=kOutput, calls=%fused_computation.1 | convolution fusion | flops 11303649280 | bytes 77594624 | tf_op jit(solution)/shard_map/dot_general | solution.py:43
  (2 shorter events, 0.0 us)
Async XLA Ops:
  7.2 52.0 %all-gather.3.cloned.1.call-start = ((), (), s32[]{:S(2)}) async-start(), calls=%async_computation.1 | async-start | bytes 2064384 | tf_op jit(solution)/shard_map/all_gather | solution.py:29
  7.9 105.1 %all-reduce.3.cloned.1.call-start = ((), (), s32[]{:S(2)}) async-start(), calls=%async_computation.2 | async-start | bytes 1048576 | tf_op jit(solution)/shard_map/psum | solution.py:32
  80.6 104.9 %all-reduce.5.cloned.1.call-start = ((), (), s32[]{:S(2)}) async-start(), calls=%async_computation.3 | async-start | bytes 131072 | tf_op jit(solution)/shard_map/psum | solution.py:33
  115.8 228.6 %reduce-scatter.2.cloned.1.call-start = ((), (), s32[]{:S(2)}) async-start(), calls=%async_computation.4 | async-start | bytes 4128768 | tf_op jit(solution)/shard_map/reduce_scatter | solution.py:36
  263.5 151.0 %all-gather.5.cloned.1.call-start = ((), (), s32[]{:S(2)}) async-start(), calls=%async_computation.5 | async-start | bytes 4128768 | tf_op jit(solution)/shard_map/all_gather | solution.py:40
  414.5 29.0 %copy-start = (f32[7168,128]{1,0:T(8,128)S(1)}, f32[7168,128]{1,0:T(8,128)}, u32[]{:S(2)}) copy-start(f32[7168,128]{1,0:T(8,128)} %all-gather.5.cloned.1.call-done) | copy-start | bytes 11010052
Sparse Core Ops, SparseCore 0:
  10.2 48.9 all-gather.2
  80.7 32.2 all-reduce.2
  117.0 68.4 all-reduce.4
  263.6 80.7 reduce-scatter.1
  346.4 67.9 all-gather.4
where the time goes:
time: 490 us; the launch traced here: 485 us
  waiting for transfers between devices  262 us (53%)
  matrix products  138 us (28%)
  blocking collectives  41.2 us (8%)
  other arithmetic  27.3 us (6%)
  between operations  14.1 us (3%)
    reduce_scatter x1, waiting for transfers between devices, local(): lax.psum_scatter(jnp.dot(columns.T, orthonormal, precision=highest), 'mp'...  80.7 us
    psum x1, waiting for transfers between devices, local(): lax.psum(jnp.dot(power_left.T, power_left, precision=highest), 'mp')  69.1 us
    dot_general x1, matrix products, local(): jnp.dot(columns.T, orthonormal, precision=highest)  51.6 us
    all_gather x1, waiting for transfers between devices, local(): lax.all_gather(factor_q, 'mp', axis=0, tiled=True).astype(jnp.float32)  51.2 us
    psum x1, blocking collectives, local(): lax.psum(jnp.sum(right_share * right_share, axis=0), ('mp', 'dp'))  41.2 us
    dot_general x1, matrix products, local(): jnp.dot(orthonormal, power_right.T, precision=highest)  34.2 us
    psum x1, waiting for transfers between devices, local(): power_left = lax.psum(power_part, 'dp')  32.3 us
    all_gather x1, waiting for transfers between devices, local(): power_right = lax.all_gather(right_share, 'mp', axis=0, tiled=True)  27.6 us
  transfers between devices with their start and end apart: 5, of which 5 were waited for; matrix products, arithmetic and copies ran while one was open for 0% of the time, Pallas kernels for 0%

commit v1 on v0

v1 whole, which is shorter than its diff:
```python
import functools
import math

import jax
import jax.numpy as jnp
from jax import lax
from jax.experimental import pallas as pl
from jax.experimental.pallas import tpu as pltpu
from jax.sharding import PartitionSpec as P

highest = lax.Precision.HIGHEST
feedback_rate = 0.05
MESH = pl.DeviceIdType.MESH
f32 = jnp.float32
bf16 = jnp.bfloat16


def make_orthonormal(power_left, gram_matrix):
    factor_low = jnp.linalg.cholesky(gram_matrix)
    return jax.scipy.linalg.solve_triangular(factor_low, power_left.T, lower=True).T


def plain(scale_factor, momentum, gradient, factor_q):
    blended = momentum + gradient.astype(f32)
    share_rows = blended.shape[1] // lax.axis_size("mp")
    power_part = jnp.dot(
        blended,
        lax.all_gather(factor_q, "mp", axis=0, tiled=True).astype(f32),
        precision=highest,
    )
    power_left = lax.psum(power_part, "dp")
    gram_matrix = lax.psum(jnp.dot(power_left.T, power_left, precision=highest), "mp")
    orthonormal = make_orthonormal(power_left, gram_matrix)
    right_share = lax.psum_scatter(
        jnp.dot(blended.T, orthonormal, precision=highest), "mp", scatter_dimension=0, tiled=True
    )
    column_sums = lax.psum(jnp.sum(right_share * right_share, axis=0), ("mp", "dp"))
    power_right = lax.all_gather(right_share, "mp", axis=0, tiled=True)
    q_new = power_right * lax.rsqrt(column_sums + 1e-06)
    q_share = lax.dynamic_slice_in_dim(q_new, lax.axis_index("mp") * share_rows, share_rows, 0)
    momentum_out = blended - feedback_rate * jnp.dot(orthonormal, power_right.T, precision=highest)
    update = (scale_factor * jnp.dot(orthonormal, q_new.T, precision=highest)).astype(bf16)
    return (momentum_out, q_share.astype(bf16), update)


def split(value):
    high = value.astype(bf16)
    return high, (value - high.astype(f32)).astype(bf16)


def factors_kernel(n, n_dp, scale_factor, mom_hbm, grad_hbm, q_ref, pr_hbm, o_ref, qout_ref,
                   b_high, b_low, q_all, mom_st, grad_st, part, part_in, left, left_t, left_cat,
                   w, right_in, left_in, gram, gram_in, aug, pr, cs, cs_in, csd_in,
                   load_sem, q_send, q_recv, dp_send, dp_recv, rs_send, rs_recv,
                   gr_send, gr_recv, ag_send, ag_recv, cs_send, cs_recv, out_sem):
    rank = q_ref.shape[1]
    share = q_ref.shape[0]
    rows = mom_hbm.shape[0]
    chunk = rows // n_dp
    half_rows = rows // 2
    half_n = n // 2
    half_rank = rank // 2
    n_bits = n.bit_length() - 1
    me = lax.axis_index("mp")
    my_dp = lax.axis_index("dp")

    def at_place(place):
        back = lax.div(place, half_n)
        return (1 - back) * (2 * place) + back * (2 * (n - 1 - place) + 1)

    odd = lax.rem(me, 2)
    pair = lax.div(me, 2)
    place = (1 - odd) * pair + odd * (n - 1 - pair)

    def owner(offset):
        return at_place(lax.rem(place + (offset + n) % n, n))

    right, left_dev = owner(1), owner(-1)

    def slot(offset):
        offset = (offset + n) % n
        if offset == 0:
            return 0
        if offset == half_n:
            return n - 1
        return 2 * offset if offset < half_n else 2 * (n - offset) - 1

    offsets = [0] * n
    for offset in range(-half_n + 1, half_n + 1):
        offsets[slot(offset)] = offset

    def partner(bit):
        step = 1 << bit
        return me + (1 - 2 * lax.rem(lax.div(me, step), 2)) * step

    def dp_peer(t):
        return lax.rem(my_dp + t, n_dp)

    def remote(src, dst, send, recv, **where):
        return pltpu.make_async_remote_copy(
            src_ref=src, dst_ref=dst, send_sem=send, recv_sem=recv, device_id=where, device_id_type=MESH
        )

    def loads(item):
        block, h = divmod(item, 2)
        cols = pl.ds(pl.multiple_of(owner(offsets[block]) * share, 128), share)
        at = pl.ds(h * half_rows, half_rows)
        return (
            pltpu.make_async_copy(mom_hbm.at[at, cols], mom_st.at[h], load_sem.at[h, 0]),
            pltpu.make_async_copy(grad_hbm.at[at, cols], grad_st.at[h], load_sem.at[h, 1]),
        )

    for item in range(2):
        for copy in loads(item):
            copy.start()

    barrier = pltpu.get_barrier_semaphore()
    greeted = [{"mp": right}, {"mp": left_dev}]
    greeted += [{"mp": partner(bit)} for bit in range(n_bits)]
    greeted += [{"dp": dp_peer(t)} for t in range(1, n_dp)]
    for where in greeted:
        pl.semaphore_signal(barrier, inc=1, device_id=where, device_id_type=MESH)
    pl.semaphore_wait(barrier, len(greeted))

    def gather_copies(s, first, blocks, half, send, recv):
        def at(offset):
            return first if offset == 0 else blocks.at[slot(offset)]

        if s < half_n - 1:
            to_right = (at(-s), blocks.at[slot(-s - 1)])
            to_left = (at(s), blocks.at[slot(s + 1)])
        else:
            low, high = pl.ds(0, half), pl.ds(half, half)
            to_right = (at(-s).at[low], blocks.at[n - 1, low])
            to_left = (at(s).at[high], blocks.at[n - 1, high])
        return (
            remote(*to_right, send.at[s, 0], recv.at[s, 0], mp=right),
            remote(*to_left, send.at[s, 1], recv.at[s, 1], mp=left_dev),
        )

    q_copies = [gather_copies(s, q_ref, q_all, share // 2, q_send, q_recv) for s in range(half_n)]
    for copy in q_copies[0]:
        copy.start()

    part[...] = jnp.zeros_like(part)
    for block in range(n):
        if block % 2 == 1:
            s = block // 2
            for copy in q_copies[s]:
                copy.wait_recv()
            if s + 1 < half_n:
                for copy in q_copies[s + 1]:
                    copy.start()
        q_block = q_ref if block == 0 else q_all.at[block]
        for h in range(2):
            item = 2 * block + h
            for copy in loads(item):
                copy.wait()

            @pl.loop(0, half_rows // chunk if half_rows >= chunk else 1)
            def _(c, block=block, h=h, q_block=q_block):
                size = min(chunk, half_rows)
                at = pl.ds(pl.multiple_of(c * size, 16), size)
                blended = mom_st[h, at, :] + grad_st[h, at, :].astype(f32)
                high, low = split(blended)
                to = pl.ds(pl.multiple_of(h * half_rows + c * size, 16), size)
                b_high[block, to, :] = high
                b_low[block, to, :] = low
                q = q_block[...]
                part[to, :] += jnp.dot(high, q, preferred_element_type=f32) + jnp.dot(
                    low, q, preferred_element_type=f32
                )

            if item + 2 < 2 * n:
                for copy in loads(item + 2):
                    copy.start()

    def rows_of(which):
        return pl.ds(pl.multiple_of(which * chunk, 16), chunk)

    scatter = [
        remote(part.at[rows_of(dp_peer(t))], part_in.at[t - 1], dp_send.at[0, t - 1], dp_recv.at[0, t - 1], dp=dp_peer(t))
        for t in range(1, n_dp)
    ]
    for copy in scatter:
        copy.start()
    for copy in scatter:
        copy.wait_recv()
    total = part[rows_of(my_dp), :]
    for t in range(n_dp - 1):
        total = total + part_in[t]
    left[rows_of(my_dp), :] = total
    handout = [
        remote(left.at[rows_of(my_dp)], left.at[rows_of(my_dp)], dp_send.at[1, t - 1], dp_recv.at[1, t - 1], dp=dp_peer(t))
        for t in range(1, n_dp)
    ]
    for copy in handout:
        copy.start()
    for copy in handout:
        copy.wait_recv()
    transposed = left[...].T
    left_t[...] = transposed
    high, low = split(transposed)
    left_cat[:rank, :] = high
    left_cat[rank:, :] = low

    def make_w(offset):
        k = slot(offset)
        b = b_high[k]
        both = jnp.dot(left_cat[...], b, preferred_element_type=f32)
        w[k] = both[:rank] + both[rank:] + jnp.dot(left_cat[:rank, :], b_low[k], preferred_element_type=f32)

    low_half, high_half = pl.ds(0, half_rank), pl.ds(half_rank, half_rank)

    def ring_copies(s):
        return (
            remote(w.at[slot(-1 - s), low_half], right_in.at[s], rs_send.at[s, 0], rs_recv.at[s, 0], mp=right),
            remote(w.at[slot(1 + s), high_half], left_in.at[s], rs_send.at[s, 1], rs_recv.at[s, 1], mp=left_dev),
        )

    def gram_copy(bit):
        return remote(gram.at[bit], gram_in.at[bit], gr_send.at[bit], gr_recv.at[bit], mp=partner(bit))

    lane = lax.broadcasted_iota(jnp.int32, (rank, rank), 1)
    line = lax.broadcasted_iota(jnp.int32, (rank, rank), 0)

    def eliminate(first, last):
        @pl.loop(first, last)
        def _(k):
            row = aug[pl.ds(k, 1), :]
            column = jnp.sum(jnp.where(lane == k, aug[:, :rank], 0.0), axis=1, keepdims=True)
            pivot = jnp.sum(jnp.where(lane[:1] == k, row[:, :rank], 0.0), axis=1, keepdims=True)
            factor = jnp.where(line[:, :1] > k, column / pivot, 0.0)
            aug[...] = aug[...] - factor * row

    spare = n - 1 - n_bits
    per_step = -(-rank // max(spare, 1))
    made = set()

    def make_once(offset):
        if slot(offset) not in made:
            made.add(slot(offset))
            make_w(offset)

    make_once(-1)
    make_once(1)
    copies = []
    for s in range(n - 1):
        if s > 0:
            before = copies[s - 1]
            before[0].wait_recv()
            k = slot(-1 - s)
            w[k, low_half, :] += right_in[s - 1]
            before[1].wait_recv()
            k = slot(1 + s)
            w[k, high_half, :] += left_in[s - 1]
        copies.append(ring_copies(s))
        for copy in copies[s]:
            copy.start()
        if s == 0:
            gram[0] = jnp.dot(left_t[...], left[...], precision=highest, preferred_element_type=f32)
            gram_copy(0).start()
        elif s <= n_bits:
            gram_copy(s - 1).wait_recv()
            gram[s] = gram[s - 1] + gram_in[s - 1]
            if s < n_bits:
                gram_copy(s).start()
        if s + 1 <= half_n:
            make_once(-2 - s)
            make_once(2 + s)
        if s == half_n - 1 or n == 2:
            make_once(0)
        if s == n_bits:
            aug[:, :rank] = gram[n_bits]
            aug[:, rank:] = jnp.where(lane == line, 1.0, 0.0)
        if s >= n_bits and (s - n_bits) * per_step < rank:
            eliminate((s - n_bits) * per_step, min(rank, (s - n_bits + 1) * per_step))
    diagonal = jnp.sum(jnp.where(lane == line, aug[:, :rank], 0.0), axis=1, keepdims=True)
    inverse_low = aug[:, rank:] / jnp.sqrt(diagonal)

    copies[n - 2][0].wait_recv()
    w[0, low_half, :] += right_in[n - 2]
    copies[n - 2][1].wait_recv()
    w[0, high_half, :] += left_in[n - 2]

    own = jnp.dot(inverse_low, w[0], precision=highest, preferred_element_type=f32)
    pr[0] = own
    ag_copies = [gather_copies(s, pr.at[0], pr, half_rank, ag_send, ag_recv) for s in range(half_n)]
    for copy in ag_copies[0]:
        copy.start()

    def keep(k):
        return pltpu.make_async_copy(pr.at[k], pr_hbm.at[owner(offsets[k])], out_sem.at[k])

    keep(0).start()

    def cs_copy(bit):
        return remote(cs.at[bit], cs_in.at[bit], cs_send.at[bit], cs_recv.at[bit], mp=partner(bit))

    def csd_copy(t):
        return remote(cs.at[n_bits], csd_in.at[t - 1], cs_send.at[n_bits + t - 1], cs_recv.at[n_bits + t - 1], dp=dp_peer(t))

    cs[0] = lax.dot_general(
        jnp.ones((8, share), f32), own * own, (((1,), (1,)), ((), ())), precision=highest, preferred_element_type=f32
    )
    cs_copy(0).start()
    ortho = lax.dot_general(
        left[...], inverse_low, (((1,), (1,)), ((), ())), precision=highest, preferred_element_type=f32
    )
    for bit in range(n_bits):
        cs_copy(bit).wait_recv()
        cs[bit + 1] = cs[bit] + cs_in[bit]
        if bit + 1 < n_bits:
            cs_copy(bit + 1).start()
        if bit < half_n - 1:
            for copy in ag_copies[bit]:
                copy.wait_recv()
            for copy in ag_copies[bit + 1]:
                copy.start()
    for t in range(1, n_dp):
        csd_copy(t).start()
    for s in range(n_bits, half_n - 1):
        for copy in ag_copies[s]:
            copy.wait_recv()
        for copy in ag_copies[s + 1]:
            copy.start()
    for k in range(1, n - 1):
        keep(k).start()
    sums = cs[n_bits]
    for t in range(1, n_dp):
        csd_copy(t).wait_recv()
    for t in range(n_dp - 1):
        sums = sums + csd_in[t]
    scale = 1.0 / jnp.sqrt(sums[:1] + 1e-06)
    o_high, o_low = split(ortho * (scale_factor * scale))
    o_ref[:, :rank] = o_high
    o_ref[:, rank : 2 * rank] = o_low
    o_ref[:, 2 * rank :] = (feedback_rate * ortho).astype(bf16)
    qout_ref[...] = (pr[0].T * scale).astype(bf16)
    for copy in ag_copies[half_n - 1]:
        copy.wait_recv()
    keep(n - 1).start()

    for group in (q_copies, ag_copies, copies):
        for pair_of in group:
            for copy in pair_of:
                copy.wait_send()
    for copy in scatter + handout:
        copy.wait_send()
    for bit in range(n_bits):
        gram_copy(bit).wait_send()
        cs_copy(bit).wait_send()
    for t in range(1, n_dp):
        csd_copy(t).wait_send()
    for k in range(n):
        keep(k).wait()


def outputs_kernel(mom_ref, grad_ref, pr_ref, o_ref, mom_out, update_out):
    rank = pr_ref.shape[1]
    high, low = split(pr_ref[0])
    product = jnp.dot(o_ref[:, : 2 * rank], jnp.concatenate([high, high], axis=0), preferred_element_type=f32)
    product += jnp.dot(o_ref[:, :rank], low, preferred_element_type=f32)
    update_out[...] = product.astype(bf16)
    blended = mom_ref[...] + grad_ref[...].astype(f32)
    mom_out[...] = blended - jnp.dot(o_ref[:, 2 * rank :], high, preferred_element_type=f32)


def fused(n, n_dp, scale_factor, momentum, gradient, factor_q):
    rows, cols = momentum.shape
    share, rank = factor_q.shape
    chunk = rows // n_dp
    n_bits = n.bit_length() - 1
    half_n = n // 2
    dma = pltpu.SemaphoreType.DMA
    vmem = pltpu.VMEM
    whole = pl.BlockSpec(memory_space=pltpu.VMEM)
    anywhere = pl.BlockSpec(memory_space=pl.ANY)
    pr, ortho, q_new = pl.pallas_call(
        functools.partial(factors_kernel, n, n_dp, scale_factor),
        out_shape=(
            jax.ShapeDtypeStruct((n, rank, share), f32),
            jax.ShapeDtypeStruct((rows, 3 * rank), bf16),
            jax.ShapeDtypeStruct((share, rank), bf16),
        ),
        in_specs=[anywhere, anywhere, whole],
        out_specs=(anywhere, whole, whole),
        scratch_shapes=[
            vmem((n, rows, share), bf16),
            vmem((n, rows, share), bf16),
            vmem((n, share, rank), bf16),
            vmem((2, rows // 2, share), f32),
            vmem((2, rows // 2, share), bf16),
            vmem((rows, rank), f32),
            vmem((n_dp - 1, chunk, rank), f32),
            vmem((rows, rank), f32),
            vmem((rank, rows), f32),
            vmem((2 * rank, rows), bf16),
            vmem((n, rank, share), f32),
            vmem((n - 1, rank // 2, share), f32),
            vmem((n - 1, rank // 2, share), f32),
            vmem((n_bits + 1, rank, rank), f32),
            vmem((n_bits, rank, rank), f32),
            vmem((rank, 2 * rank), f32),
            vmem((n, rank, share), f32),
            vmem((n_bits + 1, 8, rank), f32),
            vmem((n_bits, 8, rank), f32),
            vmem((n_dp - 1, 8, rank), f32),
            dma((2, 2)),
            dma((half_n, 2)),
            dma((half_n, 2)),
            dma((2, n_dp - 1)),
            dma((2, n_dp - 1)),
            dma((n - 1, 2)),
            dma((n - 1, 2)),
            dma((n_bits,)),
            dma((n_bits,)),
            dma((half_n, 2)),
            dma((half_n, 2)),
            dma((n_bits + n_dp - 1,)),
            dma((n_bits + n_dp - 1,)),
            dma((n,)),
        ],
        compiler_params=pltpu.CompilerParams(
            collective_id=0, has_side_effects=True, vmem_limit_bytes=60 * 1024 * 1024
        ),
    )(momentum, gradient, factor_q)
    tile = rows // 2
    momentum_out, update = pl.pallas_call(
        outputs_kernel,
        grid=(n, rows // tile),
        out_shape=(
            jax.ShapeDtypeStruct((rows, cols), f32),
            jax.ShapeDtypeStruct((rows, cols), bf16),
        ),
        in_specs=[
            pl.BlockSpec((tile, share), lambda j, i: (i, j)),
            pl.BlockSpec((tile, share), lambda j, i: (i, j)),
            pl.BlockSpec((1, rank, share), lambda j, i: (j, 0, 0)),
            pl.BlockSpec((tile, 3 * rank), lambda j, i: (i, 0)),
        ],
        out_specs=(
            pl.BlockSpec((tile, share), lambda j, i: (i, j)),
            pl.BlockSpec((tile, share), lambda j, i: (i, j)),
        ),
        compiler_params=pltpu.CompilerParams(vmem_limit_bytes=40 * 1024 * 1024),
    )(momentum, gradient, pr, ortho)
    return momentum_out, q_new, update


def solution(mesh):
    n, n_dp = mesh.shape["mp"], mesh.shape["dp"]

    def local(momentum, gradient, factor_q):
        rows, cols = momentum.shape
        share, rank = factor_q.shape
        scale_factor = math.sqrt(rows * n * cols * n_dp / rank)
        tiles = (
            share % 128 == 0
            and rank % 128 == 0
            and rows % (32 * n_dp) == 0
            and n >= 2
            and n & (n - 1) == 0
            and n_dp >= 2
            and 4 * rows * cols <= 32 * 1024 * 1024
        )
        if tiles:
            return fused(n, n_dp, scale_factor, momentum, gradient, factor_q)
        return plain(scale_factor, momentum, gradient, factor_q)

    return jax.shard_map(
        local,
        mesh=mesh,
        in_specs=(P("mp", "dp"), P("mp", "dp"), P(("dp", "mp"), None)),
        out_specs=(P("mp", "dp"), P(("dp", "mp"), None), P("mp", "dp")),
        check_vma=False,
    )
```

time: 490 us -> 175 us (0.36); the launches traced: 485 us -> 175 us
  waiting for transfers between devices: 262 us -> 0 us
  Pallas kernels: 0 us -> 170 us
  matrix products: 138 us -> 0 us
  blocking collectives: 41.2 us -> 0 us
  other arithmetic: 27.3 us -> 0 us
  between operations: 14.1 us -> 0.65 us
    pallas_call x0 -> x2, Pallas kernels: none -> 170 us  [the longest x1 134 us: fused(): pl.pallas_call(functools.partial(factors_kernel, n, n_dp, scale_factor),...]
    dot_general x5 -> x0, matrix products: 136 us -> none  [the longest x1 51.6 us: local(): jnp.dot(columns.T, orthonormal, precision=highest)]
    psum x2 -> x0, waiting for transfers between devices: 101 us -> none  [the longest x1 69.1 us: local(): lax.psum(jnp.dot(power_left.T, power_left, precision=highest), 'mp')]
    reduce_scatter x1 -> x0, waiting for transfers between devices: 80.7 us -> none  [local(): lax.psum_scatter(jnp.dot(columns.T, orthonormal, precision=highest), 'mp'...]
    all_gather x2 -> x0, waiting for transfers between devices: 78.9 us -> none  [the longest x1 51.2 us: local(): lax.all_gather(factor_q, 'mp', axis=0, tiled=True).astype(jnp.float32)]
    psum x1 -> x0, blocking collectives: 41.2 us -> none  [local(): lax.psum(jnp.sum(right_share * right_share, axis=0), ('mp', 'dp'))]
    another operation x5 -> x0, other arithmetic: 22.9 us -> none  [the longest x3 12.4 us: make_orthonormal(): factor_low = jnp.linalg.cholesky(gram_matrix)]
  transfers between devices with their start and end apart: 5 -> 0, of which waited for: 5 -> 0; matrix products, arithmetic and copies ran while one was open for 0% -> 0% of each run, Pallas kernels for 0% -> 0%
where the time goes in v1:
time: 175 us
  Pallas kernels  170 us (97%)
  local copies, waits for them, and re-layouts  3.86 us (2%)
    pallas_call x1, Pallas kernels, fused(): pl.pallas_call(functools.partial(factors_kernel, n, n_dp, scale_factor),...  134 us
    pallas_call x1, Pallas kernels, fused(): pl.pallas_call(outputs_kernel, grid=(n, rows // tile), out_shape=(jax.Sha...  35.9 us
    unnamed x7, local copies, waits for them, and re-layouts  3.86 us

profile of v1, /device:TPU:0, one launch (start us, length us, event | category | flops | bytes accessed | tf_op | source)
XLA Modules:
  0.0 174.8 jit_solution(3316036306278721819)
XLA Ops:
  0.6 134.4 %shard_map.58 = (f32[8,128,896]{2,1,0:T(8,128)}, bf16[1024,384]{1,0:T(8,128)(2,1)}, bf16[896,128]{1,0:T(8,128)(2,1)}) custom-call(f32[1024,7168]{1,0:T(8,128)} %mom_ref.1, bf16[1024,7168]{1,0:T(8,128)(2,1)} %grad_ref.1, bf16[896,128]{1,0:T(8,128)(2,1)} %q_ref.1), custom_call_target="tpu_custom_call" | custom-call | tf_op jit(solution)/shard_map/pallas_call | solution.py:379
  135.0 0.0 copy-start
  135.0 2.0 %copy-done = f32[8,128,896]{2,1,0:T(8,128)S(1)} copy-done((f32[8,128,896]{2,1,0:T(8,128)S(1)}, f32[8,128,896]{2,1,0:T(8,128)}, u32[]{:S(2)}) %copy-start) | copy-done | bytes 3670040
  137.1 0.0 copy-start.1
  137.1 1.1 copy-done.1
  138.2 0.0 copy-start.2
  138.2 35.9 %shard_map.59 = (f32[1024,7168]{1,0:T(8,128)}, bf16[1024,7168]{1,0:T(8,128)(2,1)}) custom-call(f32[1024,7168]{1,0:T(8,128)} %mom_ref.1, bf16[1024,7168]{1,0:T(8,128)(2,1)} %grad_ref.1, f32[8,128,896]{2,1,0:T(8,128)S(1)} %copy-done, bf16[1024,384]{1,0:T(8,128)(2,1)S(1)} %copy-done.1), custom_call_target="tpu_custom_call" | custom-call | tf_op jit(solution)/shard_map/pallas_call | solution.py:429
  174.1 0.0 copy-done.2
  174.1 0.7 copy.7
Async XLA Ops:
  135.0 2.0 %copy-start = (f32[8,128,896]{2,1,0:T(8,128)S(1)}, f32[8,128,896]{2,1,0:T(8,128)}, u32[]{:S(2)}) copy-start(f32[8,128,896]{2,1,0:T(8,128)} %get-tuple-element.8.pr_ref) | copy-start | bytes 11010052
  137.1 1.1 copy-start.1
  138.2 36.0 %copy-start.2 = (bf16[896,128]{1,0:T(8,128)(2,1)S(1)}, bf16[896,128]{1,0:T(8,128)(2,1)}, u32[]{:S(2)}) copy-start(bf16[896,128]{1,0:T(8,128)(2,1)} %get-tuple-element.17) | copy-start | bytes 688132

commit v2 on v1

--- a/solution.py
+++ b/solution.py
@@ -48,7 +48,7 @@
     return high, (value - high.astype(f32)).astype(bf16)
 
 
-def factors_kernel(n, n_dp, scale_factor, mom_hbm, grad_hbm, q_ref, pr_hbm, o_ref, qout_ref,
+def factors_kernel(n, n_dp, scale_factor, mom_hbm, grad_hbm, q_ref, pr_own, pr_before, pr_after, o_ref, qout_ref,
                    b_high, b_low, q_all, mom_st, grad_st, part, part_in, left, left_t, left_cat,
                    w, right_in, left_in, gram, gram_in, aug, pr, cs, cs_in, csd_in,
                    load_sem, q_send, q_recv, dp_send, dp_recv, rs_send, rs_recv,
@@ -175,29 +175,29 @@
                 for copy in loads(item + 2):
                     copy.start()
 
+    core = lax.rem(my_dp, 2)
+    mate = my_dp + 1 - 2 * core
+
     def rows_of(which):
-        return pl.ds(pl.multiple_of(which * chunk, 16), chunk)
-
-    scatter = [
-        remote(part.at[rows_of(dp_peer(t))], part_in.at[t - 1], dp_send.at[0, t - 1], dp_recv.at[0, t - 1], dp=dp_peer(t))
-        for t in range(1, n_dp)
-    ]
-    for copy in scatter:
+        return pl.ds(pl.multiple_of(which * half_rows, 16), half_rows)
+
+    mine = rows_of(core)
+    dp_copies = [remote(part.at[rows_of(1 - core)], part_in.at[0], dp_send.at[0], dp_recv.at[0], dp=mate)]
+    dp_copies[0].start()
+    dp_copies[0].wait_recv()
+    part[mine, :] += part_in[0]
+    for t in range(1, n_dp // 2):
+        copy = remote(part.at[mine], part_in.at[t], dp_send.at[t], dp_recv.at[t], dp=dp_peer(2 * t))
         copy.start()
-    for copy in scatter:
-        copy.wait_recv()
-    total = part[rows_of(my_dp), :]
-    for t in range(n_dp - 1):
+        dp_copies.append(copy)
+    total = part[mine, :]
+    for t in range(1, n_dp // 2):
+        dp_copies[t].wait_recv()
         total = total + part_in[t]
-    left[rows_of(my_dp), :] = total
-    handout = [
-        remote(left.at[rows_of(my_dp)], left.at[rows_of(my_dp)], dp_send.at[1, t - 1], dp_recv.at[1, t - 1], dp=dp_peer(t))
-        for t in range(1, n_dp)
-    ]
-    for copy in handout:
-        copy.start()
-    for copy in handout:
-        copy.wait_recv()
+    left[mine, :] = total
+    handout = remote(left.at[mine], left.at[mine], dp_send.at[n_dp // 2], dp_recv.at[n_dp // 2], dp=mate)
+    handout.start()
+    handout.wait_recv()
     transposed = left[...].T
     left_t[...] = transposed
     high, low = split(transposed)
@@ -285,12 +285,12 @@
 
     own = jnp.dot(inverse_low, w[0], precision=highest, preferred_element_type=f32)
     pr[0] = own
-    ag_copies = [gather_copies(s, pr.at[0], pr, half_rank, ag_send, ag_recv) for s in range(half_n)]
-    for copy in ag_copies[0]:
+    ag_copies = gather_copies(0, pr.at[0], pr, half_rank, ag_send, ag_recv)
+    for copy in ag_copies:
         copy.start()
 
     def keep(k):
-        return pltpu.make_async_copy(pr.at[k], pr_hbm.at[owner(offsets[k])], out_sem.at[k])
+        return pltpu.make_async_copy(pr.at[k], (pr_own, pr_before, pr_after)[k], out_sem.at[k])
 
     keep(0).start()
 
@@ -312,20 +312,8 @@
         cs[bit + 1] = cs[bit] + cs_in[bit]
         if bit + 1 < n_bits:
             cs_copy(bit + 1).start()
-        if bit < half_n - 1:
-            for copy in ag_copies[bit]:
-                copy.wait_recv()
-            for copy in ag_copies[bit + 1]:
-                copy.start()
     for t in range(1, n_dp):
         csd_copy(t).start()
-    for s in range(n_bits, half_n - 1):
-        for copy in ag_copies[s]:
-            copy.wait_recv()
-        for copy in ag_copies[s + 1]:
-            copy.start()
-    for k in range(1, n - 1):
-        keep(k).start()
     sums = cs[n_bits]
     for t in range(1, n_dp):
         csd_copy(t).wait_recv()
@@ -337,28 +325,39 @@
     o_ref[:, rank : 2 * rank] = o_low
     o_ref[:, 2 * rank :] = (feedback_rate * ortho).astype(bf16)
     qout_ref[...] = (pr[0].T * scale).astype(bf16)
-    for copy in ag_copies[half_n - 1]:
+    for copy, k in zip(ag_copies, (1, 2)):
         copy.wait_recv()
-    keep(n - 1).start()
-
-    for group in (q_copies, ag_copies, copies):
+        keep(k).start()
+
+    for group in (q_copies, [ag_copies], copies):
         for pair_of in group:
             for copy in pair_of:
                 copy.wait_send()
-    for copy in scatter + handout:
+    for copy in dp_copies + [handout]:
         copy.wait_send()
     for bit in range(n_bits):
         gram_copy(bit).wait_send()
         cs_copy(bit).wait_send()
     for t in range(1, n_dp):
         csd_copy(t).wait_send()
-    for k in range(n):
+    for k in range(3):
         keep(k).wait()
 
 
-def outputs_kernel(mom_ref, grad_ref, pr_ref, o_ref, mom_out, update_out):
-    rank = pr_ref.shape[1]
-    high, low = split(pr_ref[0])
+def outputs_kernel(pieces, idx_ref, mom_ref, grad_ref, o_ref, *refs):
+    del idx_ref
+    block = pl.program_id(0)
+    mom_out, update_out = refs[-2:]
+    values, first = [], 0
+    for count in pieces:
+        parts = [ref[...] for ref in refs[first : first + count]]
+        values.append(parts[0] if count == 1 else jnp.concatenate(parts, axis=0))
+        first += count
+    value = values[0]
+    for k in range(1, len(values)):
+        value = jnp.where(block == k, values[k], value)
+    rank = value.shape[0]
+    high, low = split(value)
     product = jnp.dot(o_ref[:, : 2 * rank], jnp.concatenate([high, high], axis=0), preferred_element_type=f32)
     product += jnp.dot(o_ref[:, :rank], low, preferred_element_type=f32)
     update_out[...] = product.astype(bf16)
@@ -366,25 +365,64 @@
     mom_out[...] = blended - jnp.dot(o_ref[:, 2 * rank :], high, preferred_element_type=f32)
 
 
+def write_outputs(blocks, owners, momentum, gradient, ortho, outputs):
+    rows, cols = momentum.shape
+    pieces = tuple(len(parts) for parts in blocks)
+    flat = [part for parts in blocks for part in parts]
+    share = flat[0].shape[1]
+    rank = ortho.shape[1] // 3
+    tile = rows // 4
+    def columns():
+        return pl.BlockSpec((tile, share), lambda j, i, idx: (i, idx[j]))
+
+    whole = pl.BlockSpec(memory_space=pltpu.VMEM)
+    anywhere = pl.BlockSpec(memory_space=pl.ANY)
+    given = [] if outputs is None else list(outputs)
+    kernel = functools.partial(outputs_kernel, pieces)
+    first = 4 + len(flat)
+    area = len(blocks) * rows * share
+    return pl.pallas_call(
+        kernel,
+        grid_spec=pltpu.PrefetchScalarGridSpec(
+            num_scalar_prefetch=1,
+            grid=(len(blocks), rows // tile),
+            in_specs=[
+                columns(),
+                columns(),
+                pl.BlockSpec((tile, 3 * rank), lambda j, i, idx: (i, 0)),
+                *[whole for _ in flat],
+                *[anywhere for _ in given],
+            ],
+            out_specs=(columns(), columns()),
+        ),
+        out_shape=(
+            jax.ShapeDtypeStruct((rows, cols), f32),
+            jax.ShapeDtypeStruct((rows, cols), bf16),
+        ),
+        input_output_aliases={first: 0, first + 1: 1} if given else {},
+        cost_estimate=pl.CostEstimate(flops=8 * rank * area, bytes_accessed=12 * area, transcendentals=0),
+        compiler_params=pltpu.CompilerParams(vmem_limit_bytes=60 * 1024 * 1024),
+    )(owners, momentum, gradient, ortho, *flat, *given)
+
+
 def fused(n, n_dp, scale_factor, momentum, gradient, factor_q):
     rows, cols = momentum.shape
     share, rank = factor_q.shape
-    chunk = rows // n_dp
     n_bits = n.bit_length() - 1
     half_n = n // 2
     dma = pltpu.SemaphoreType.DMA
     vmem = pltpu.VMEM
     whole = pl.BlockSpec(memory_space=pltpu.VMEM)
     anywhere = pl.BlockSpec(memory_space=pl.ANY)
-    pr, ortho, q_new = pl.pallas_call(
+    own, before, after, ortho, q_new = pl.pallas_call(
         functools.partial(factors_kernel, n, n_dp, scale_factor),
         out_shape=(
-            jax.ShapeDtypeStruct((n, rank, share), f32),
+            *[jax.ShapeDtypeStruct((rank, share), f32)] * 3,
             jax.ShapeDtypeStruct((rows, 3 * rank), bf16),
             jax.ShapeDtypeStruct((share, rank), bf16),
         ),
         in_specs=[anywhere, anywhere, whole],
-        out_specs=(anywhere, whole, whole),
+        out_specs=(anywhere, anywhere, anywhere, whole, whole),
         scratch_shapes=[
             vmem((n, rows, share), bf16),
             vmem((n, rows, share), bf16),
@@ -392,7 +430,7 @@
             vmem((2, rows // 2, share), f32),
             vmem((2, rows // 2, share), bf16),
             vmem((rows, rank), f32),
-            vmem((n_dp - 1, chunk, rank), f32),
+            vmem((n_dp // 2, rows // 2, rank), f32),
             vmem((rows, rank), f32),
             vmem((rank, rows), f32),
             vmem((2 * rank, rows), bf16),
@@ -402,49 +440,59 @@
             vmem((n_bits + 1, rank, rank), f32),
             vmem((n_bits, rank, rank), f32),
             vmem((rank, 2 * rank), f32),
-            vmem((n, rank, share), f32),
+            vmem((3, rank, share), f32),
             vmem((n_bits + 1, 8, rank), f32),
             vmem((n_bits, 8, rank), f32),
             vmem((n_dp - 1, 8, rank), f32),
             dma((2, 2)),
             dma((half_n, 2)),
             dma((half_n, 2)),
-            dma((2, n_dp - 1)),
-            dma((2, n_dp - 1)),
+            dma((n_dp // 2 + 1,)),
+            dma((n_dp // 2 + 1,)),
             dma((n - 1, 2)),
             dma((n - 1, 2)),
             dma((n_bits,)),
             dma((n_bits,)),
-            dma((half_n, 2)),
-            dma((half_n, 2)),
+            dma((1, 2)),
+            dma((1, 2)),
             dma((n_bits + n_dp - 1,)),
             dma((n_bits + n_dp - 1,)),
-            dma((n,)),
+            dma((3,)),
         ],
         compiler_params=pltpu.CompilerParams(
             collective_id=0, has_side_effects=True, vmem_limit_bytes=60 * 1024 * 1024
         ),
     )(momentum, gradient, factor_q)
-    tile = rows // 2
-    momentum_out, update = pl.pallas_call(
-        outputs_kernel,
-        grid=(n, rows // tile),
-        out_shape=(
-            jax.ShapeDtypeStruct((rows, cols), f32),
-            jax.ShapeDtypeStruct((rows, cols), bf16),
-        ),
-        in_specs=[
-            pl.BlockSpec((tile, share), lambda j, i: (i, j)),
-            pl.BlockSpec((tile, share), lambda j, i: (i, j)),
-            pl.BlockSpec((1, rank, share), lambda j, i: (j, 0, 0)),
-            pl.BlockSpec((tile, 3 * rank), lambda j, i: (i, 0)),
-        ],
-        out_specs=(
-            pl.BlockSpec((tile, share), lambda j, i: (i, j)),
-            pl.BlockSpec((tile, share), lambda j, i: (i, j)),
-        ),
-        compiler_params=pltpu.CompilerParams(vmem_limit_bytes=40 * 1024 * 1024),
-    )(momentum, gradient, pr, ortho)
+
+    ring = [2 * p if p < half_n else 2 * (n - 1 - p) + 1 for p in range(n)]
+    up = [(ring[p], ring[(p + 1) % n]) for p in range(n)]
+    down = [(b, a) for a, b in up]
+    me = lax.axis_index("mp")
+    odd = lax.rem(me, 2)
+    place = (1 - odd) * lax.div(me, 2) + odd * (n - 1 - lax.div(me, 2))
+
+    def owners(*offsets):
+        at = lax.rem(place + n + jnp.array(offsets, jnp.int32), jnp.int32(n))
+        back = lax.div(at, jnp.int32(half_n))
+        return (1 - back) * (2 * at) + back * (2 * (n - 1 - at) + 1)
+
+    outputs = None
+    ready, at = [(own,), (before,), (after,)], owners(0, -1, 1)
+    for s in range(1, half_n):
+        if s < half_n - 1:
+            before = lax.ppermute(before, "mp", up)
+            after = lax.ppermute(after, "mp", down)
+            coming, then = [(before,), (after,)], owners(-1 - s, 1 + s)
+        else:
+            low = lax.ppermute(before[: rank // 2], "mp", up)
+            high = lax.ppermute(after[rank // 2 :], "mp", down)
+            coming, then = [(low, high)], owners(half_n)
+        outputs = write_outputs(ready, at, momentum, gradient, ortho, outputs)
+        outputs, coming = lax.optimization_barrier((outputs, coming))
+        if s < half_n - 1:
+            (before,), (after,) = coming
+        ready, at = coming, then
+    momentum_out, update = write_outputs(ready, at, momentum, gradient, ortho, outputs)
     return momentum_out, q_new, update
 
 
@@ -459,9 +507,9 @@
             share % 128 == 0
             and rank % 128 == 0
             and rows % (32 * n_dp) == 0
-            and n >= 2
+            and n >= 4
             and n & (n - 1) == 0
-            and n_dp >= 2
+            and n_dp % 2 == 0
             and 4 * rows * cols <= 32 * 1024 * 1024
         )
         if tiles:

time: 175 us -> 174 us (level)
  Pallas kernels: 170 us -> 163 us
  starting transfers between devices: 0 us -> 6.23 us
  local copies, waits for them, and re-layouts: 3.86 us -> 1.5 us
    pallas_call x1, Pallas kernels: 134 us -> 112 us  [fused(): pl.pallas_call(functools.partial(factors_kernel, n, n_dp, scale_factor),...]
    pallas_call x1 -> x4, Pallas kernels: 35.9 us -> 51.3 us  [write_outputs(): pl.pallas_call(kernel, grid_spec=pltpu.PrefetchScalarGridSpec(num_scalar_...]
    ppermute x0 -> x6, starting transfers between devices: none -> 6.23 us  [the longest x2 3.98 us: fused(): after = lax.ppermute(after, 'mp', down)]
    unnamed x7 -> x21, local copies, waits for them, and re-layouts: 3.86 us -> 1.46 us
  transfers between devices with their start and end apart: 0 -> 6, of which waited for: 0 -> 0; matrix products, arithmetic and copies ran while one was open for 0% -> 1% of each run, Pallas kernels for 0% -> 26%
where the time goes in v2:
time: 174 us; the launch traced here: 173 us
  Pallas kernels  163 us (94%)
  starting transfers between devices  6.23 us (4%)
    pallas_call x1, Pallas kernels, fused(): pl.pallas_call(functools.partial(factors_kernel, n, n_dp, scale_factor),...  112 us
    pallas_call x4, Pallas kernels, write_outputs(): pl.pallas_call(kernel, grid_spec=pltpu.PrefetchScalarGridSpec(num_scalar_...  51.3 us
    ppermute x2, starting transfers between devices, fused(): after = lax.ppermute(after, 'mp', down)  3.98 us
  transfers between devices with their start and end apart: 6, of which 0 were waited for; matrix products, arithmetic and copies ran while one was open for 1% of the time, Pallas kernels for 26%

profile of v2, /device:TPU:0, one launch (start us, length us, event | category | flops | bytes accessed | tf_op | source)
XLA Modules:
  0.0 172.9 jit_solution(14135016548122649962)
XLA Ops:
  0.6 0.0 copy-start.9
  0.6 111.9 %shard_map.94 = (f32[128,896]{1,0:T(8,128)}, f32[128,896]{1,0:T(8,128)}, f32[128,896]{1,0:T(8,128)}, bf16[1024,384]{1,0:T(8,128)(2,1)}, bf16[896,128]{1,0:T(8,128)(2,1)}) custom-call(f32[1024,7168]{1,0:T(8,128)} %mom_ref.7, bf16[1024,7168]{1,0:T(8,128)(2,1)} %grad_ref.7, bf16[896,128]{1,0:T(8,128)(2,1)} %q_ref.1), custom_call_target="tpu_custom_call" | custom-call | tf_op jit(solution)/shard_map/pallas_call | solution.py:417
  112.5 0.0 copy-start.7
  112.5 0.0 copy-start.8
  112.5 0.1 collective-permute-start
  112.6 2.0 %collective-permute-start.1 = (f32[128,896]{1,0:T(8,128)}, f32[128,896]{1,0:T(8,128)S(1)}, u32[]{:S(2)}, u32[]{:S(2)}) collective-permute-start(f32[128,896]{1,0:T(8,128)} %get-tuple-element.31.refs_2_), channel_id=1, source_target_pairs={{8,0},{16,8},{24,16},{28,24},{20,28},{12,20},{4,12},{0,4},{9,1},{1... | collective-permute-start | bytes 1376264 | tf_op jit(solution)/shard_map/ppermute | solution.py:484
  114.6 0.0 copy-done.9
  114.6 0.5 multiply_add_fusion.idx_ref
  115.1 18.7 %shard_map.95 = (f32[1024,7168]{1,0:T(8,128)}, bf16[1024,7168]{1,0:T(8,128)(2,1)}) custom-call(s32[3]{0:T(128)} %multiply_add_fusion.idx_ref, f32[1024,7168]{1,0:T(8,128)} %mom_ref.7, bf16[1024,7168]{1,0:T(8,128)(2,1)} %grad_ref.7, bf16[1024,384]{1,0:T(8,128)(2,1)} %get-tuple-element.28.o_ref, f32[128,896]{1,0:T(8,128)} %get-tuple-element.29.refs_0_, ...), custom_call_target="tpu_custom_call" | custom-call | flops 2818572288 | bytes 33030144 | tf_op jit(solution)/shard_map/pallas_call | solution.py:384
  133.8 0.0 collective-permute-done.refs_0_
  133.9 0.0 copy-start.2
  133.9 0.0 collective-permute-done.1.refs_1_
  133.9 0.0 copy-start.3
  133.9 0.1 collective-permute-start.2
  134.0 2.0 %collective-permute-start.3 = (f32[128,896]{1,0:T(8,128)S(1)}, f32[128,896]{1,0:T(8,128)S(1)}, u32[]{:S(2)}, u32[]{:S(2)}) collective-permute-start(f32[128,896]{1,0:T(8,128)S(1)} %collective-permute-done.1.refs_1_), channel_id=1, source_target_pairs={{8,0},{16,8},{24,16},{28,24},{20,28},{12,20},{4,12},{0,4},{9,1},{1... | collective-permute-start | bytes 1376264 | tf_op jit(solution)/shard_map/ppermute | solution.py:484
  136.0 0.0 copy-done.7
  136.0 0.0 copy-done.8
  136.0 0.6 multiply_add_fusion.1
  136.6 0.0 copy-done.2
  136.6 0.0 copy-done.3
  136.6 13.0 %shard_map.96 = (f32[1024,7168]{1,0:T(8,128)}, bf16[1024,7168]{1,0:T(8,128)(2,1)}) custom-call(s32[2]{0:T(128)} %get-tuple-element.53.idx_ref, f32[1024,7168]{1,0:T(8,128)} %mom_ref.7, bf16[1024,7168]{1,0:T(8,128)(2,1)} %grad_ref.7, bf16[1024,384]{1,0:T(8,128)(2,1)} %get-tuple-element.28.o_ref, ...), custom_call_target="tpu_custom_call", output_to_operand_aliasing={{0}: (6, {}), {1}: (7, {})} | custom-call | flops 1879048192 | bytes 22020096 | tf_op jit(solution)/shard_map/pallas_call | solution.py:384
  149.6 0.0 collective-permute-done.2.refs_0_
  149.6 0.0 copy-start
  149.6 0.0 collective-permute-done.3.refs_1_
  149.6 0.0 copy-start.1
  149.7 0.1 collective-permute-start.4
  149.8 2.0 %collective-permute-start.5 = (f32[64,896]{1,0:T(8,128)S(1)}, f32[64,896]{1,0:T(8,128)S(1)}, u32[]{:S(2)}, u32[]{:S(2)}) collective-permute-start(f32[64,896]{1,0:T(8,128)S(1)} %slice.7), channel_id=1, source_target_pairs={{8,0},{16,8},{24,16},{28,24},{20,28},{12,20},{4,12},{0,4},{9,1},{1... | collective-permute-start | bytes 688136 | tf_op jit(solution)/shard_map/ppermute | solution.py:488
  151.8 0.0 copy-done
  151.8 0.0 copy-done.1
  151.8 13.0 %shard_map.97 = (f32[1024,7168]{1,0:T(8,128)}, bf16[1024,7168]{1,0:T(8,128)(2,1)}) custom-call(s32[2]{0:T(128)} %get-tuple-element.54.idx_ref, f32[1024,7168]{1,0:T(8,128)} %mom_ref.7, bf16[1024,7168]{1,0:T(8,128)(2,1)} %grad_ref.7, bf16[1024,384]{1,0:T(8,128)(2,1)} %get-tuple-element.28.o_ref, ...), custom_call_target="tpu_custom_call", output_to_operand_aliasing={{0}: (6, {}), {1}: (7, {})} | custom-call | flops 1879048192 | bytes 22020096 | tf_op jit(solution)/shard_map/pallas_call | solution.py:384
  164.8 0.0 collective-permute-done.4.refs_0_
  164.8 0.0 copy-start.4
  164.8 0.0 collective-permute-done.5.refs_1_
  164.9 0.0 copy-start.5
  164.9 0.7 copy-done.4
  165.5 0.1 copy-done.5
  165.6 0.0 copy-start.6
  165.6 6.6 %shard_map.98 = (f32[1024,7168]{1,0:T(8,128)}, bf16[1024,7168]{1,0:T(8,128)(2,1)}) custom-call(s32[1]{0:T(128)S(6)} %add.60.idx_ref, f32[1024,7168]{1,0:T(8,128)} %mom_ref.7, bf16[1024,7168]{1,0:T(8,128)(2,1)} %grad_ref.7, bf16[1024,384]{1,0:T(8,128)(2,1)} %get-tuple-element.28.o_ref, ...), custom_call_target="tpu_custom_call", output_to_operand_aliasing={{0}: (6, {}), {1}: (7, {})} | custom-call | flops 939524096 | bytes 11010048 | tf_op jit(solution)/shard_map/pallas_call | solution.py:384
  172.2 0.0 copy-done.6
  172.2 0.7 copy.23
  (2 shorter events, 0.0 us)
Async XLA Ops:
  0.6 114.0 %copy-start.9 = (s32[3]{0:T(128)S(1)}, s32[3]{0:T(128)}, u32[]{:S(2)}) copy-start(s32[3]{0:T(128)} %constant.66.clone) | copy-start | bytes 40
  112.5 23.5 %copy-start.7 = (s32[2]{0:T(128)S(1)}, s32[2]{0:T(128)}, u32[]{:S(2)}) copy-start(s32[2]{0:T(128)} %constant.68.clone) | copy-start | bytes 28
  112.5 23.4 %copy-start.8 = (s32[2]{0:T(128)S(1)}, s32[2]{0:T(128)}, u32[]{:S(2)}) copy-start(s32[2]{0:T(128)} %constant.67.clone) | copy-start | bytes 28
  112.5 21.3 %collective-permute-start = (f32[128,896]{1,0:T(8,128)}, f32[128,896]{1,0:T(8,128)S(1)}, u32[]{:S(2)}, u32[]{:S(2)}) collective-permute-start(f32[128,896]{1,0:T(8,128)} %get-tuple-element.30.refs_1_), channel_id=1, source_target_pairs={{0,8},{8,16},{16,24},{24,28},{28,20},{20,12},{12,4},{4,0},{1,9},{9... | collective-permute-start | bytes 1376264 | tf_op jit(solution)/shard_map/ppermute | solution.py:483
  112.6 21.3 %collective-permute-start.1 = (f32[128,896]{1,0:T(8,128)}, f32[128,896]{1,0:T(8,128)S(1)}, u32[]{:S(2)}, u32[]{:S(2)}) collective-permute-start(f32[128,896]{1,0:T(8,128)} %get-tuple-element.31.refs_2_), channel_id=1, source_target_pairs={{8,0},{16,8},{24,16},{28,24},{20,28},{12,20},{4,12},{0,4},{9,1},{1... | collective-permute-start | bytes 1376264 | tf_op jit(solution)/shard_map/ppermute | solution.py:484
  133.9 2.7 %copy-start.2 = (f32[128,896]{1,0:T(8,128)}, f32[128,896]{1,0:T(8,128)S(1)}, u32[]{:S(2)}) copy-start(f32[128,896]{1,0:T(8,128)S(1)} %collective-permute-done.refs_0_) | copy-start | bytes 1376260
  133.9 2.7 %copy-start.3 = (f32[128,896]{1,0:T(8,128)}, f32[128,896]{1,0:T(8,128)S(1)}, u32[]{:S(2)}) copy-start(f32[128,896]{1,0:T(8,128)S(1)} %collective-permute-done.1.refs_1_) | copy-start | bytes 1376260
  133.9 15.7 %collective-permute-start.2 = (f32[128,896]{1,0:T(8,128)S(1)}, f32[128,896]{1,0:T(8,128)S(1)}, u32[]{:S(2)}, u32[]{:S(2)}) collective-permute-start(f32[128,896]{1,0:T(8,128)S(1)} %collective-permute-done.refs_0_), channel_id=1, source_target_pairs={{0,8},{8,16},{16,24},{24,28},{28,20},{20,12},{12,4},{4,0},{1,9},{9... | collective-permute-start | bytes 1376264 | tf_op jit(solution)/shard_map/ppermute | solution.py:483
  134.0 15.6 %collective-permute-start.3 = (f32[128,896]{1,0:T(8,128)S(1)}, f32[128,896]{1,0:T(8,128)S(1)}, u32[]{:S(2)}, u32[]{:S(2)}) collective-permute-start(f32[128,896]{1,0:T(8,128)S(1)} %collective-permute-done.1.refs_1_), channel_id=1, source_target_pairs={{8,0},{16,8},{24,16},{28,24},{20,28},{12,20},{4,12},{0,4},{9,1},{1... | collective-permute-start | bytes 1376264 | tf_op jit(solution)/shard_map/ppermute | solution.py:484
  149.6 2.2 %copy-start = (f32[128,896]{1,0:T(8,128)}, f32[128,896]{1,0:T(8,128)S(1)}, u32[]{:S(2)}) copy-start(f32[128,896]{1,0:T(8,128)S(1)} %collective-permute-done.2.refs_0_) | copy-start | bytes 1376260
  149.6 2.1 %copy-start.1 = (f32[128,896]{1,0:T(8,128)}, f32[128,896]{1,0:T(8,128)S(1)}, u32[]{:S(2)}) copy-start(f32[128,896]{1,0:T(8,128)S(1)} %collective-permute-done.3.refs_1_) | copy-start | bytes 1376260
  149.7 15.1 %collective-permute-start.4 = (f32[64,896]{1,0:T(8,128)S(1)}, f32[64,896]{1,0:T(8,128)S(1)}, u32[]{:S(2)}, u32[]{:S(2)}) collective-permute-start(f32[64,896]{1,0:T(8,128)S(1)} %slice.6), channel_id=1, source_target_pairs={{0,8},{8,16},{16,24},{24,28},{28,20},{20,12},{12,4},{4,0},{1,9},{9... | collective-permute-start | bytes 688136 | tf_op jit(solution)/shard_map/ppermute | solution.py:487
  149.8 15.0 %collective-permute-start.5 = (f32[64,896]{1,0:T(8,128)S(1)}, f32[64,896]{1,0:T(8,128)S(1)}, u32[]{:S(2)}, u32[]{:S(2)}) collective-permute-start(f32[64,896]{1,0:T(8,128)S(1)} %slice.7), channel_id=1, source_target_pairs={{8,0},{16,8},{24,16},{28,24},{20,28},{12,20},{4,12},{0,4},{9,1},{1... | collective-permute-start | bytes 688136 | tf_op jit(solution)/shard_map/ppermute | solution.py:488
  164.8 0.7 copy-start.4
  164.9 0.7 copy-start.5
  165.6 6.6 %copy-start.6 = (bf16[896,128]{1,0:T(8,128)(2,1)S(1)}, bf16[896,128]{1,0:T(8,128)(2,1)}, u32[]{:S(2)}) copy-start(bf16[896,128]{1,0:T(8,128)(2,1)} %get-tuple-element.59) | copy-start | bytes 688132

commit v3 on v2

--- a/solution.py
+++ b/solution.py
@@ -347,22 +347,29 @@
 def outputs_kernel(pieces, idx_ref, mom_ref, grad_ref, o_ref, *refs):
     del idx_ref
     block = pl.program_id(0)
-    mom_out, update_out = refs[-2:]
-    values, first = [], 0
-    for count in pieces:
-        parts = [ref[...] for ref in refs[first : first + count]]
-        values.append(parts[0] if count == 1 else jnp.concatenate(parts, axis=0))
-        first += count
-    value = values[0]
-    for k in range(1, len(values)):
-        value = jnp.where(block == k, values[k], value)
-    rank = value.shape[0]
-    high, low = split(value)
-    product = jnp.dot(o_ref[:, : 2 * rank], jnp.concatenate([high, high], axis=0), preferred_element_type=f32)
-    product += jnp.dot(o_ref[:, :rank], low, preferred_element_type=f32)
+    mom_out, update_out, twice, low_part = refs[-4:]
+    rank = low_part.shape[0]
+
+    @pl.when(pl.program_id(1) == 0)
+    def _():
+        values, first = [], 0
+        for count in pieces:
+            parts = [ref[...] for ref in refs[first : first + count]]
+            values.append(parts[0] if count == 1 else jnp.concatenate(parts, axis=0))
+            first += count
+        value = values[0]
+        for k in range(1, len(values)):
+            value = jnp.where(block == k, values[k], value)
+        high, low = split(value)
+        twice[:rank, :] = high
+        twice[rank:, :] = high
+        low_part[...] = low
+
+    product = jnp.dot(o_ref[:, : 2 * rank], twice[...], preferred_element_type=f32)
+    product += jnp.dot(o_ref[:, :rank], low_part[...], preferred_element_type=f32)
     update_out[...] = product.astype(bf16)
     blended = mom_ref[...] + grad_ref[...].astype(f32)
-    mom_out[...] = blended - jnp.dot(o_ref[:, 2 * rank :], high, preferred_element_type=f32)
+    mom_out[...] = blended - jnp.dot(o_ref[:, 2 * rank :], twice[:rank, :], preferred_element_type=f32)
 
 
 def write_outputs(blocks, owners, momentum, gradient, ortho, outputs):
@@ -371,7 +378,7 @@
     flat = [part for parts in blocks for part in parts]
     share = flat[0].shape[1]
     rank = ortho.shape[1] // 3
-    tile = rows // 4
+    tile = rows // 2
     def columns():
         return pl.BlockSpec((tile, share), lambda j, i, idx: (i, idx[j]))
 
@@ -394,6 +401,7 @@
                 *[anywhere for _ in given],
             ],
             out_specs=(columns(), columns()),
+            scratch_shapes=[pltpu.VMEM((2 * rank, share), bf16), pltpu.VMEM((rank, share), bf16)],
         ),
         out_shape=(
             jax.ShapeDtypeStruct((rows, cols), f32),

time: 174 us -> 165 us (0.948)
  Pallas kernels: 163 us -> 155 us
    pallas_call x4, Pallas kernels: 51.3 us -> 43.6 us  [write_outputs(): pl.pallas_call(kernel, grid_spec=pltpu.PrefetchScalarGridSpec(num_scalar_...]
  transfers between devices with their start and end apart: 6 -> 6, of which waited for: 0 -> 0; matrix products, arithmetic and copies ran while one was open for 1% -> 1% of each run, Pallas kernels for 26% -> 23%
where the time goes in v3:
time: 165 us
  Pallas kernels  155 us (94%)
  starting transfers between devices  6.23 us (4%)
    pallas_call x1, Pallas kernels, fused(): pl.pallas_call(functools.partial(factors_kernel, n, n_dp, scale_factor),...  112 us
    pallas_call x4, Pallas kernels, write_outputs(): pl.pallas_call(kernel, grid_spec=pltpu.PrefetchScalarGridSpec(num_scalar_...  43.6 us
    ppermute x2, starting transfers between devices, fused(): after = lax.ppermute(after, 'mp', down)  3.98 us
  transfers between devices with their start and end apart: 6, of which 0 were waited for; matrix products, arithmetic and copies ran while one was open for 1% of the time, Pallas kernels for 23%

profile of v3, /device:TPU:0, one launch (start us, length us, event | category | flops | bytes accessed | tf_op | source)
XLA Modules:
  0.0 165.1 jit_solution(2399351133924484842)
XLA Ops:
  0.6 0.0 copy-start.9
  0.6 111.9 %shard_map.94 = (f32[128,896]{1,0:T(8,128)}, f32[128,896]{1,0:T(8,128)}, f32[128,896]{1,0:T(8,128)}, bf16[1024,384]{1,0:T(8,128)(2,1)}, bf16[896,128]{1,0:T(8,128)(2,1)}) custom-call(f32[1024,7168]{1,0:T(8,128)} %mom_ref.7, bf16[1024,7168]{1,0:T(8,128)(2,1)} %grad_ref.7, bf16[896,128]{1,0:T(8,128)(2,1)} %q_ref.1), custom_call_target="tpu_custom_call" | custom-call | tf_op jit(solution)/shard_map/pallas_call | solution.py:425
  112.5 0.0 copy-start.7
  112.5 0.0 copy-start.8
  112.5 0.1 collective-permute-start
  112.6 2.0 %collective-permute-start.1 = (f32[128,896]{1,0:T(8,128)}, f32[128,896]{1,0:T(8,128)S(1)}, u32[]{:S(2)}, u32[]{:S(2)}) collective-permute-start(f32[128,896]{1,0:T(8,128)} %get-tuple-element.31.refs_2_), channel_id=1, source_target_pairs={{8,0},{16,8},{24,16},{28,24},{20,28},{12,20},{4,12},{0,4},{9,1},{1... | collective-permute-start | bytes 1376264 | tf_op jit(solution)/shard_map/ppermute | solution.py:492
  114.6 0.0 copy-done.9
  114.6 0.5 multiply_add_fusion.idx_ref
  115.1 15.6 %shard_map.95 = (f32[1024,7168]{1,0:T(8,128)}, bf16[1024,7168]{1,0:T(8,128)(2,1)}) custom-call(s32[3]{0:T(128)} %multiply_add_fusion.idx_ref, f32[1024,7168]{1,0:T(8,128)} %mom_ref.7, bf16[1024,7168]{1,0:T(8,128)(2,1)} %grad_ref.7, bf16[1024,384]{1,0:T(8,128)(2,1)} %get-tuple-element.28.o_ref, f32[128,896]{1,0:T(8,128)} %get-tuple-element.29.refs_0_, ...), custom_call_target="tpu_custom_call" | custom-call | flops 2818572288 | bytes 33030144 | tf_op jit(solution)/shard_map/pallas_call | solution.py:391
  130.7 0.0 collective-permute-done.refs_0_
  130.7 0.0 copy-start.2
  130.8 0.0 collective-permute-done.1.refs_1_
  130.8 0.0 copy-start.3
  130.8 0.1 collective-permute-start.2
  130.9 2.0 %collective-permute-start.3 = (f32[128,896]{1,0:T(8,128)S(1)}, f32[128,896]{1,0:T(8,128)S(1)}, u32[]{:S(2)}, u32[]{:S(2)}) collective-permute-start(f32[128,896]{1,0:T(8,128)S(1)} %collective-permute-done.1.refs_1_), channel_id=1, source_target_pairs={{8,0},{16,8},{24,16},{28,24},{20,28},{12,20},{4,12},{0,4},{9,1},{1... | collective-permute-start | bytes 1376264 | tf_op jit(solution)/shard_map/ppermute | solution.py:492
  132.9 0.0 copy-done.7
  132.9 0.0 copy-done.8
  132.9 0.6 multiply_add_fusion.1
  133.5 0.0 copy-done.2
  133.5 0.0 copy-done.3
  133.5 11.2 %shard_map.96 = (f32[1024,7168]{1,0:T(8,128)}, bf16[1024,7168]{1,0:T(8,128)(2,1)}) custom-call(s32[2]{0:T(128)} %get-tuple-element.53.idx_ref, f32[1024,7168]{1,0:T(8,128)} %mom_ref.7, bf16[1024,7168]{1,0:T(8,128)(2,1)} %grad_ref.7, bf16[1024,384]{1,0:T(8,128)(2,1)} %get-tuple-element.28.o_ref, ...), custom_call_target="tpu_custom_call", output_to_operand_aliasing={{0}: (6, {}), {1}: (7, {})} | custom-call | flops 1879048192 | bytes 22020096 | tf_op jit(solution)/shard_map/pallas_call | solution.py:391
  144.7 0.0 collective-permute-done.2.refs_0_
  144.7 0.0 copy-start
  144.7 0.0 collective-permute-done.3.refs_1_
  144.7 0.0 copy-start.1
  144.8 0.3 collective-permute-start.4
  145.0 1.8 %collective-permute-start.5 = (f32[64,896]{1,0:T(8,128)S(1)}, f32[64,896]{1,0:T(8,128)S(1)}, u32[]{:S(2)}, u32[]{:S(2)}) collective-permute-start(f32[64,896]{1,0:T(8,128)S(1)} %slice.7), channel_id=1, source_target_pairs={{8,0},{16,8},{24,16},{28,24},{20,28},{12,20},{4,12},{0,4},{9,1},{1... | collective-permute-start | bytes 688136 | tf_op jit(solution)/shard_map/ppermute | solution.py:496
  146.8 0.0 copy-done
  146.8 0.0 copy-done.1
  146.8 11.2 %shard_map.97 = (f32[1024,7168]{1,0:T(8,128)}, bf16[1024,7168]{1,0:T(8,128)(2,1)}) custom-call(s32[2]{0:T(128)} %get-tuple-element.54.idx_ref, f32[1024,7168]{1,0:T(8,128)} %mom_ref.7, bf16[1024,7168]{1,0:T(8,128)(2,1)} %grad_ref.7, bf16[1024,384]{1,0:T(8,128)(2,1)} %get-tuple-element.28.o_ref, ...), custom_call_target="tpu_custom_call", output_to_operand_aliasing={{0}: (6, {}), {1}: (7, {})} | custom-call | flops 1879048192 | bytes 22020096 | tf_op jit(solution)/shard_map/pallas_call | solution.py:391
  158.0 0.0 collective-permute-done.4.refs_0_
  158.0 0.0 copy-start.4
  158.0 0.0 collective-permute-done.5.refs_1_
  158.1 0.0 copy-start.5
  158.1 0.7 copy-done.4
  158.7 0.1 copy-done.5
  158.8 0.0 copy-start.6
  158.8 5.7 %shard_map.98 = (f32[1024,7168]{1,0:T(8,128)}, bf16[1024,7168]{1,0:T(8,128)(2,1)}) custom-call(s32[1]{0:T(128)S(6)} %add.60.idx_ref, f32[1024,7168]{1,0:T(8,128)} %mom_ref.7, bf16[1024,7168]{1,0:T(8,128)(2,1)} %grad_ref.7, bf16[1024,384]{1,0:T(8,128)(2,1)} %get-tuple-element.28.o_ref, ...), custom_call_target="tpu_custom_call", output_to_operand_aliasing={{0}: (6, {}), {1}: (7, {})} | custom-call | flops 939524096 | bytes 11010048 | tf_op jit(solution)/shard_map/pallas_call | solution.py:391
  164.5 0.0 copy-done.6
  164.5 0.7 copy.23
  (2 shorter events, 0.0 us)
Async XLA Ops:
  0.6 114.0 %copy-start.9 = (s32[3]{0:T(128)S(1)}, s32[3]{0:T(128)}, u32[]{:S(2)}) copy-start(s32[3]{0:T(128)} %constant.66.clone) | copy-start | bytes 40
  112.5 20.3 %copy-start.7 = (s32[2]{0:T(128)S(1)}, s32[2]{0:T(128)}, u32[]{:S(2)}) copy-start(s32[2]{0:T(128)} %constant.68.clone) | copy-start | bytes 28
  112.5 20.3 %copy-start.8 = (s32[2]{0:T(128)S(1)}, s32[2]{0:T(128)}, u32[]{:S(2)}) copy-start(s32[2]{0:T(128)} %constant.67.clone) | copy-start | bytes 28
  112.5 18.2 %collective-permute-start = (f32[128,896]{1,0:T(8,128)}, f32[128,896]{1,0:T(8,128)S(1)}, u32[]{:S(2)}, u32[]{:S(2)}) collective-permute-start(f32[128,896]{1,0:T(8,128)} %get-tuple-element.30.refs_1_), channel_id=1, source_target_pairs={{0,8},{8,16},{16,24},{24,28},{28,20},{20,12},{12,4},{4,0},{1,9},{9... | collective-permute-start | bytes 1376264 | tf_op jit(solution)/shard_map/ppermute | solution.py:491
  112.6 18.2 %collective-permute-start.1 = (f32[128,896]{1,0:T(8,128)}, f32[128,896]{1,0:T(8,128)S(1)}, u32[]{:S(2)}, u32[]{:S(2)}) collective-permute-start(f32[128,896]{1,0:T(8,128)} %get-tuple-element.31.refs_2_), channel_id=1, source_target_pairs={{8,0},{16,8},{24,16},{28,24},{20,28},{12,20},{4,12},{0,4},{9,1},{1... | collective-permute-start | bytes 1376264 | tf_op jit(solution)/shard_map/ppermute | solution.py:492
  130.7 2.7 %copy-start.2 = (f32[128,896]{1,0:T(8,128)}, f32[128,896]{1,0:T(8,128)S(1)}, u32[]{:S(2)}) copy-start(f32[128,896]{1,0:T(8,128)S(1)} %collective-permute-done.refs_0_) | copy-start | bytes 1376260
  130.8 2.7 %copy-start.3 = (f32[128,896]{1,0:T(8,128)}, f32[128,896]{1,0:T(8,128)S(1)}, u32[]{:S(2)}) copy-start(f32[128,896]{1,0:T(8,128)S(1)} %collective-permute-done.1.refs_1_) | copy-start | bytes 1376260
  130.8 13.9 %collective-permute-start.2 = (f32[128,896]{1,0:T(8,128)S(1)}, f32[128,896]{1,0:T(8,128)S(1)}, u32[]{:S(2)}, u32[]{:S(2)}) collective-permute-start(f32[128,896]{1,0:T(8,128)S(1)} %collective-permute-done.refs_0_), channel_id=1, source_target_pairs={{0,8},{8,16},{16,24},{24,28},{28,20},{20,12},{12,4},{4,0},{1,9},{9... | collective-permute-start | bytes 1376264 | tf_op jit(solution)/shard_map/ppermute | solution.py:491
  130.9 13.8 %collective-permute-start.3 = (f32[128,896]{1,0:T(8,128)S(1)}, f32[128,896]{1,0:T(8,128)S(1)}, u32[]{:S(2)}, u32[]{:S(2)}) collective-permute-start(f32[128,896]{1,0:T(8,128)S(1)} %collective-permute-done.1.refs_1_), channel_id=1, source_target_pairs={{8,0},{16,8},{24,16},{28,24},{20,28},{12,20},{4,12},{0,4},{9,1},{1... | collective-permute-start | bytes 1376264 | tf_op jit(solution)/shard_map/ppermute | solution.py:492
  144.7 2.2 %copy-start = (f32[128,896]{1,0:T(8,128)}, f32[128,896]{1,0:T(8,128)S(1)}, u32[]{:S(2)}) copy-start(f32[128,896]{1,0:T(8,128)S(1)} %collective-permute-done.2.refs_0_) | copy-start | bytes 1376260
  144.7 2.1 %copy-start.1 = (f32[128,896]{1,0:T(8,128)}, f32[128,896]{1,0:T(8,128)S(1)}, u32[]{:S(2)}) copy-start(f32[128,896]{1,0:T(8,128)S(1)} %collective-permute-done.3.refs_1_) | copy-start | bytes 1376260
  144.8 13.3 %collective-permute-start.4 = (f32[64,896]{1,0:T(8,128)S(1)}, f32[64,896]{1,0:T(8,128)S(1)}, u32[]{:S(2)}, u32[]{:S(2)}) collective-permute-start(f32[64,896]{1,0:T(8,128)S(1)} %slice.6), channel_id=1, source_target_pairs={{0,8},{8,16},{16,24},{24,28},{28,20},{20,12},{12,4},{4,0},{1,9},{9... | collective-permute-start | bytes 688136 | tf_op jit(solution)/shard_map/ppermute | solution.py:495
  145.0 13.0 %collective-permute-start.5 = (f32[64,896]{1,0:T(8,128)S(1)}, f32[64,896]{1,0:T(8,128)S(1)}, u32[]{:S(2)}, u32[]{:S(2)}) collective-permute-start(f32[64,896]{1,0:T(8,128)S(1)} %slice.7), channel_id=1, source_target_pairs={{8,0},{16,8},{24,16},{28,24},{20,28},{12,20},{4,12},{0,4},{9,1},{1... | collective-permute-start | bytes 688136 | tf_op jit(solution)/shard_map/ppermute | solution.py:496
  158.0 0.7 copy-start.4
  158.1 0.7 copy-start.5
  158.8 5.7 %copy-start.6 = (bf16[896,128]{1,0:T(8,128)(2,1)S(1)}, bf16[896,128]{1,0:T(8,128)(2,1)}, u32[]{:S(2)}) copy-start(bf16[896,128]{1,0:T(8,128)(2,1)} %get-tuple-element.59) | copy-start | bytes 688132
